TPU v7x, 128 devices: a whole 4x4x4 slice. The times are simulated.
128 devices in a mesh: row: 8 (over y, core), col: 16 (over z, x).
Axes of the slice: x: 4, y: 4, z: 4, core: 2. Of those that a mesh axis runs over, the one named last changes fastest.
Arguments:
- block_x: float32 [64, 98304], P(None, ('row', 'col')), may hold values from -6 to 6
- block_p: float32 [64, 98304], P(None, ('row', 'col')), may hold values from -6 to 6
- tile_rows: int32 [8, 16, 576], P('row', 'col'), may hold values from 0 to 95, as said below
- tile_cols: int32 [8, 16, 576], P('row', 'col'), may hold values from 0 to 47, as said below
- tile_count: int32 [8, 16], P('row', 'col'), may hold values from 1 to 576, as said below
- tile_vals: bfloat16 [8, 16, 576, 128, 128], P('row', 'col'), may hold values from -0.125 to 0.125
Outputs:
- residual: float32 [64, 98304], P(None, ('row', 'col'))
- image_r: float32 [64, 98304], P(None, ('row', 'col'))
- gram_a: float32 [192, 192], replicated
- gram_b: float32 [192, 192], replicated
Inputs may be any that keep to these rules, and one draw needn't show every extreme that they name: `tile_rows`: within one grid cell the live slots name distinct tiles, all with i <= j; slots at and beyond the cell's count are ignored. `tile_cols`: paired with tile_rows slot by slot. `tile_count`: some grid cell is full in every draw.
All inputs are finite; a program needn't handle non-finite values.
Results may differ from a plain program's by a relative error of at most 0.0035.
Values may be sent and summed in bfloat16 or wider, within the bound.
A program may use at most 128 MiB of HBM per device.

v0:
```python
import math
import jax
import jax.numpy as jnp
from jax import lax
from jax.sharding import PartitionSpec as P


def apply_graph(vectors, tile_rows, tile_cols, live_count, tile_vals):
    vec_width = vectors.shape[0]
    tile_size = tile_vals.shape[-1]
    row_range = lax.all_gather(vectors, "col", axis=1, tiled=True)
    col_group = lax.all_gather(vectors, "row", axis=1, tiled=True)
    row_blocks = row_range.reshape(vec_width, -1, tile_size)
    col_blocks = col_group.reshape(vec_width, -1, tile_size)
    group_size = math.gcd(tile_vals.shape[0], 64)
    offsets = jnp.arange(group_size, dtype=jnp.int32)
    turn_count = (live_count + group_size - 1) // group_size

    def slot_group(turn_index):
        first_slot = turn_index * group_size
        row_index = lax.dynamic_slice_in_dim(tile_rows, first_slot, group_size)
        col_index = lax.dynamic_slice_in_dim(tile_cols, first_slot, group_size)
        values = lax.dynamic_slice_in_dim(tile_vals, first_slot, group_size, 0)
        live_slots = first_slot + offsets < live_count
        return (row_index, col_index, values, live_slots)

    def turn(turn_index, totals):
        row_totals, col_totals = totals
        row_index, col_index, values, live_slots = slot_group(turn_index)
        values = jnp.where(live_slots[:, None, None], values, jnp.zeros_like(values))
        col_inputs = jnp.take(col_blocks, col_index, axis=1)
        row_inputs = jnp.take(row_blocks, row_index, axis=1)
        forward = jnp.einsum("wgb,gab->wga", col_inputs, values, preferred_element_type=jnp.float32)
        backward = jnp.einsum(
            "wga,gab->wgb", row_inputs, values, preferred_element_type=jnp.float32
        )
        return (row_totals.at[:, row_index].add(forward), col_totals.at[:, col_index].add(backward))

    start_rows = jnp.zeros(row_blocks.shape, jnp.float32)
    start_cols = jnp.zeros(col_blocks.shape, jnp.float32)
    row_totals, col_totals = lax.fori_loop(0, turn_count, turn, (start_rows, start_cols))
    own_rows = lax.psum_scatter(
        row_totals.reshape(vec_width, -1), "col", scatter_dimension=1, tiled=True
    )
    own_cols = lax.psum_scatter(
        col_totals.reshape(vec_width, -1), "row", scatter_dimension=1, tiled=True
    )
    return own_rows + own_cols


def per_device(block_x, block_p, tile_rows, tile_cols, tile_count, tile_vals):
    highest = lax.Precision.HIGHEST
    width_k = block_x.shape[0]
    node_count = block_x.shape[1] * lax.axis_size("row") * lax.axis_size("col")
    slot_rows = tile_rows[0, 0]
    slot_cols = tile_cols[0, 0]
    live_count = tile_count[0, 0]
    slot_vals = tile_vals[0, 0]

    def product(left, right):
        return (
            jnp.dot(left, right.T, precision=highest, preferred_element_type=jnp.float32)
            / node_count
        )

    gram_x = lax.psum(product(block_x, block_x), ("row", "col"))
    cholesky_factor = jnp.linalg.cholesky(gram_x)
    orthonormal = lax.linalg.triangular_solve(cholesky_factor, block_x, left_side=True, lower=True)
    ortho_low = orthonormal.astype(jnp.bfloat16)
    dir_low = block_p.astype(jnp.bfloat16)
    both_images = apply_graph(
        jnp.concatenate([ortho_low, dir_low], axis=0), slot_rows, slot_cols, live_count, slot_vals
    )
    image_x = both_images[:width_k]
    image_p = both_images[width_k:]
    rayleigh = lax.psum(product(orthonormal, image_x), ("row", "col"))
    residual = image_x - jnp.dot(
        rayleigh.T, orthonormal, precision=highest, preferred_element_type=jnp.float32
    )
    residual_low = residual.astype(jnp.bfloat16)
    image_r = apply_graph(residual_low, slot_rows, slot_cols, live_count, slot_vals)
    basis = jnp.concatenate([orthonormal, residual, block_p], axis=0)
    images = jnp.concatenate([image_x, image_r, image_p], axis=0)
    gram_a, gram_b = lax.psum((product(basis, images), product(basis, basis)), ("row", "col"))
    return (residual, image_r, gram_a, gram_b)


def solution(mesh):
    in_specs = (
        P(None, ("row", "col")),
        P(None, ("row", "col")),
        P("row", "col", None),
        P("row", "col", None),
        P("row", "col"),
        P("row", "col", None, None, None),
    )
    out_specs = (P(None, ("row", "col")), P(None, ("row", "col")), P(), P())
    return jax.shard_map(
        per_device, mesh=mesh, in_specs=in_specs, out_specs=out_specs, check_vma=False
    )
```

profile of v0, /device:TPU:1, one launch (start us, length us, event | category | flops | bytes accessed | tf_op | source)
XLA Modules:
  0.0 1301.9 jit_solution(9293041823528149920)
XLA Ops:
  8.4 68.9 %psum.28 = f32[64,64]{0,1:T(8,128)S(1)} all-reduce(f32[64,64]{0,1:T(8,128)S(1)} %convolution_multiply_fusion.3), channel_id=1, replica_groups=mesh['row'=8,'col'=16] {'row','col'}, use_global_device_ids=true, to_apply=%region_0.0 | all-reduce | flops 4096 | bytes 32768 | tf_op jit(solution)/shard_map/psum | solution.py:66
  93.1 19.8 %all-gather.4.cloned.1.call-done = bf16[128,6144]{1,0:T(8,128)(2,1)} async-done(((bf16[128,768]{1,0:T(8,128)(2,1)}), bf16[128,6144]{1,0:T(8,128)(2,1)}) %all-gather.4.cloned.1.call-update) | async-done | bytes 1572880 | tf_op jit(solution)/shard_map/all_gather | solution.py:12
  115.9 47.5 %all-gather.6.cloned.1.call-done = bf16[128,12288]{1,0:T(8,128)(2,1)} async-done(((bf16[128,768]{1,0:T(8,128)(2,1)}), bf16[128,12288]{1,0:T(8,128)(2,1)}) %all-gather.6.cloned.1.call-update) | async-done | bytes 3145744 | tf_op jit(solution)/shard_map/all_gather | solution.py:11
  171.6 290.6 %while.26 = (s32[]{:T(128)}, f32[128,96,128]{2,0,1:T(8,128)}, f32[128,48,128]{2,0,1:T(8,128)S(1)}, s32[]{:T(128)}, s32[576]{0:T(1024)S(1)}, /*index=5*/s32[]{:T(...) while((s32[]{:T(128)}, f32[128,96,128]{2,0,1:T(8,128)}, ...), condition=%wide.region_6.7_spmd.clone, body=%wide.region_3.6_spmd.clone.sunk | while | flops 543165312 | bytes 50343056 | solution.py:41
  181.7 13.6 %scatter_fusion = f32[128,96,128]{2,0,1:T(8,128)} fusion(f32[128,96,128]{2,0,1:T(8,128)} %get-tuple-element.407, s32[64]{0:T(128)S(1)} %get-tuple-element.374, f32[64,128,128]{2,1,0:T(8,128)} %fusion.80), kind=kCustom, calls=%fused_computation.4.clone.clone.1 | custom fusion | flops 1048576 | bytes 12583168 | tf_op jit(solution)/shard_map/while/body/scatter-add | solution.py:37
  223.2 13.6 %scatter_fusion = f32[128,96,128]{2,0,1:T(8,128)} fusion(f32[128,96,128]{2,0,1:T(8,128)} %get-tuple-element.407, s32[64]{0:T(128)S(1)} %get-tuple-element.374, f32[64,128,128]{2,1,0:T(8,128)} %fusion.80), kind=kCustom, calls=%fused_computation.4.clone.clone.1 | custom fusion | flops 1048576 | bytes 12583168 | tf_op jit(solution)/shard_map/while/body/scatter-add | solution.py:37
  264.8 13.6 %scatter_fusion = f32[128,96,128]{2,0,1:T(8,128)} fusion(f32[128,96,128]{2,0,1:T(8,128)} %get-tuple-element.407, s32[64]{0:T(128)S(1)} %get-tuple-element.374, f32[64,128,128]{2,1,0:T(8,128)} %fusion.80), kind=kCustom, calls=%fused_computation.4.clone.clone.1 | custom fusion | flops 1048576 | bytes 12583168 | tf_op jit(solution)/shard_map/while/body/scatter-add | solution.py:37
  306.3 13.5 %scatter_fusion = f32[128,96,128]{2,0,1:T(8,128)} fusion(f32[128,96,128]{2,0,1:T(8,128)} %get-tuple-element.407, s32[64]{0:T(128)S(1)} %get-tuple-element.374, f32[64,128,128]{2,1,0:T(8,128)} %fusion.80), kind=kCustom, calls=%fused_computation.4.clone.clone.1 | custom fusion | flops 1048576 | bytes 12583168 | tf_op jit(solution)/shard_map/while/body/scatter-add | solution.py:37
  347.7 13.6 %scatter_fusion = f32[128,96,128]{2,0,1:T(8,128)} fusion(f32[128,96,128]{2,0,1:T(8,128)} %get-tuple-element.407, s32[64]{0:T(128)S(1)} %get-tuple-element.374, f32[64,128,128]{2,1,0:T(8,128)} %fusion.80), kind=kCustom, calls=%fused_computation.4.clone.clone.1 | custom fusion | flops 1048576 | bytes 12583168 | tf_op jit(solution)/shard_map/while/body/scatter-add | solution.py:37
  389.2 13.6 %scatter_fusion = f32[128,96,128]{2,0,1:T(8,128)} fusion(f32[128,96,128]{2,0,1:T(8,128)} %get-tuple-element.407, s32[64]{0:T(128)S(1)} %get-tuple-element.374, f32[64,128,128]{2,1,0:T(8,128)} %fusion.80), kind=kCustom, calls=%fused_computation.4.clone.clone.1 | custom fusion | flops 1048576 | bytes 12583168 | tf_op jit(solution)/shard_map/while/body/scatter-add | solution.py:37
  430.7 13.6 %scatter_fusion = f32[128,96,128]{2,0,1:T(8,128)} fusion(f32[128,96,128]{2,0,1:T(8,128)} %get-tuple-element.407, s32[64]{0:T(128)S(1)} %get-tuple-element.374, f32[64,128,128]{2,1,0:T(8,128)} %fusion.80), kind=kCustom, calls=%fused_computation.4.clone.clone.1 | custom fusion | flops 1048576 | bytes 12583168 | tf_op jit(solution)/shard_map/while/body/scatter-add | solution.py:37
  470.4 106.4 %reduce-scatter.7.cloned.1.call-done = f32[128,768]{1,0:T(8,128)} async-done(((f32[128,6144]{1,0:T(8,128)}), f32[128,768]{1,0:T(8,128)}) %reduce-scatter.7.cloned.1.call-update) | async-done | bytes 393232 | tf_op jit(solution)/shard_map/reduce_scatter | solution.py:45
  576.8 85.4 %reduce-scatter.5.cloned.1.call-done = f32[128,768]{1,0:T(8,128)} async-done(((f32[128,12288]{1,0:T(8,128)}), f32[128,768]{1,0:T(8,128)}) %reduce-scatter.5.cloned.1.call-update) | async-done | bytes 393232 | tf_op jit(solution)/shard_map/reduce_scatter | solution.py:42
  663.6 65.7 %psum.29 = f32[64,64]{0,1:T(8,128)S(1)} all-reduce(f32[64,64]{0,1:T(8,128)S(1)} %convolution_multiply_fusion.2), channel_id=1, replica_groups=mesh['row'=8,'col'=16] {'row','col'}, use_global_device_ids=true, to_apply=%region_9.10 | all-reduce | flops 4096 | bytes 32768 | tf_op jit(solution)/shard_map/psum | solution.py:76
  730.4 14.3 %all_gather.14 = bf16[64,6144]{1,0:T(8,128)(2,1)S(1)} all-gather(bf16[64,768]{1,0:T(8,128)(2,1)} %get-tuple-element.250), channel_id=1, replica_groups=mesh['row'=8,'col'=16] {'row'}, dimensions={1}, use_global_device_ids=true | all-gather | bytes 884736 | tf_op jit(solution)/shard_map/all_gather | solution.py:12
  745.8 24.0 %all-gather.8.cloned.1.call-done = bf16[64,12288]{1,0:T(8,128)(2,1)} async-done(((bf16[64,768]{1,0:T(8,128)(2,1)}), bf16[64,12288]{1,0:T(8,128)(2,1)}) %all-gather.8.cloned.1.call-update) | async-done | bytes 1572880 | tf_op jit(solution)/shard_map/all_gather | solution.py:11
  776.2 198.4 %while.27 = (s32[]{:T(128)}, f32[64,96,128]{2,0,1:T(8,128)}, f32[64,48,128]{2,0,1:T(8,128)}, s32[]{:T(128)}, s32[576]{0:T(1024)S(1)}, /*index=5*/s32[]{:T(128)},...) while((s32[]{:T(128)}, f32[64,96,128]{2,0,1:T(8,128)}, ...), condition=%wide.region_13.14_spmd.clone, body=%wide.region_10.13_spmd.clone.sunk | while | flops 272632704 | bytes 27274384 | solution.py:41
  782.0 9.0 scatter_fusion.2
  795.5 9.0 scatter_fusion.3
  810.4 9.0 scatter_fusion.2
  838.7 9.0 scatter_fusion.2
  852.2 9.0 scatter_fusion.3
  880.5 9.0 scatter_fusion.3
  895.3 9.0 scatter_fusion.2
  908.9 9.0 scatter_fusion.3
  923.6 9.1 scatter_fusion.2
  937.2 9.0 scatter_fusion.3
  952.0 9.0 scatter_fusion.2
  965.5 9.0 scatter_fusion.3
  981.7 80.2 %reduce-scatter.11.cloned.1.call-done = f32[64,768]{1,0:T(8,128)} async-done(((f32[64,6144]{1,0:T(8,128)}), f32[64,768]{1,0:T(8,128)}) %reduce-scatter.11.cloned.1.call-update) | async-done | bytes 196624 | tf_op jit(solution)/shard_map/reduce_scatter | solution.py:45
  1061.9 79.4 %reduce-scatter.9.cloned.1.call-done = f32[64,768]{1,0:T(8,128)} async-done(((f32[64,12288]{1,0:T(8,128)}), f32[64,768]{1,0:T(8,128)}) %reduce-scatter.9.cloned.1.call-update) | async-done | bytes 196624 | tf_op jit(solution)/shard_map/reduce_scatter | solution.py:42
  1143.7 148.1 %all-reduce.3.cloned.1.call-done = (f32[192,192]{1,0:T(8,128)}, f32[192,192]{1,0:T(8,128)}) async-done(((f32[192,192]{1,0:T(8,128)}, f32[192,192]{1,0:T(8,128)}), (f32[192,192]{1,0:T(8,128)}, f32[192,192]{1,0:T(8,128)})) %all-reduce.3.cloned.1.call-update) | async-done | bytes 294928 | tf_op jit(solution)/shard_map/psum | solution.py:84
  (191 shorter events, 343.4 us)
Async XLA Ops:
  7.2 0.9 copy-start
  7.2 85.8 %copy-start.8 = (s32[1,1,576]{2,1,0:T(1,128)S(1)}, s32[1,1,576]{2,1,0:T(1,128)}, u32[]{:S(2)}) copy-start(s32[1,1,576]{2,1,0:T(1,128)} %param.12) | copy-start | bytes 6916
  7.2 85.8 %copy-start.9 = (s32[1,1,576]{2,1,0:T(1,128)S(1)}, s32[1,1,576]{2,1,0:T(1,128)}, u32[]{:S(2)}) copy-start(s32[1,1,576]{2,1,0:T(1,128)} %param.13) | copy-start | bytes 6916
  7.2 105.7 %all-gather.4.cloned.1.call-start = ((), (), s32[]{:S(2)}) async-start(), calls=%async_computation.4 | async-start | bytes 1769472 | tf_op jit(solution)/shard_map/all_gather | solution.py:12
  91.5 71.8 %all-gather.6.cloned.1.call-start = ((), (), s32[]{:S(2)}) async-start(), calls=%async_computation.5 | async-start | bytes 3342336 | tf_op jit(solution)/shard_map/all_gather | solution.py:11
  92.3 484.5 %reduce-scatter.7.cloned.1.call-start = ((), (), s32[]{:S(2)}) async-start(), calls=%async_computation.7 | async-start | bytes 3538944 | tf_op jit(solution)/shard_map/reduce_scatter | solution.py:45
  464.2 198.0 %reduce-scatter.5.cloned.1.call-start = ((), (), s32[]{:S(2)}) async-start(), calls=%async_computation.6 | async-start | bytes 6684672 | tf_op jit(solution)/shard_map/reduce_scatter | solution.py:42
  470.3 299.4 %all-gather.8.cloned.1.call-start = ((), (), s32[]{:S(2)}) async-start(), calls=%async_computation.8 | async-start | bytes 1671168 | tf_op jit(solution)/shard_map/all_gather | solution.py:11
  663.3 109.5 %copy-start.3 = (f32[128,768]{1,0:T(8,128)}, f32[128,768]{1,0:T(8,128)S(1)}, u32[]{:S(2)}) copy-start(f32[128,768]{1,0:T(8,128)S(1)} %add.116) | copy-start | bytes 1179652
  730.3 331.6 %reduce-scatter.11.cloned.1.call-start = ((), (), s32[]{:S(2)}) async-start(), calls=%async_computation.10 | async-start | bytes 1769472 | tf_op jit(solution)/shard_map/reduce_scatter | solution.py:45
  974.6 2.9 copy-start.2
  977.4 163.9 %reduce-scatter.9.cloned.1.call-start = ((), (), s32[]{:S(2)}) async-start(), calls=%async_computation.9 | async-start | bytes 3342336 | tf_op jit(solution)/shard_map/reduce_scatter | solution.py:42
  979.3 0.9 copy-start.5
  979.3 1.0 copy-start.6
  979.3 2.3 copy-start.4
  979.3 312.4 %all-reduce.3.cloned.1.call-start = ((), (), s32[]{:S(2)}) async-start(), calls=%async_computation.11 | async-start | bytes 786432 | tf_op jit(solution)/shard_map/psum | solution.py:84
  980.3 314.7 %copy-start.1 = (f32[64,768]{1,0:T(8,128)S(1)}, f32[64,768]{1,0:T(8,128)}, u32[]{:S(2)}) copy-start(f32[64,768]{1,0:T(8,128)} %param.10) | copy-start | bytes 589828
  1142.3 152.7 %copy-start.7 = (f32[64,768]{1,0:T(8,128)}, f32[64,768]{1,0:T(8,128)S(1)}, u32[]{:S(2)}) copy-start(f32[64,768]{1,0:T(8,128)S(1)} %add.117) | copy-start | bytes 589828
Sparse Core Ops, SparseCore 0:
  91.7 21.1 all-gather.3
  115.6 47.6 all-gather.5
  464.3 112.4 reduce-scatter.6
  580.0 82.0 reduce-scatter.4
  730.4 39.2 all-gather.7
  977.5 84.3 reduce-scatter.10
  1065.2 76.0 reduce-scatter.8
  1146.6 145.1 all-reduce.2
where the time goes:
time: 1310 us; the launch traced here: 1300 us
  waiting for transfers between devices  591 us (45%)
  other arithmetic  309 us (24%)
  blocking collectives  149 us (11%)
  local copies, waits for them, and re-layouts  118 us (9%)
  matrix products  118 us (9%)
  between operations  15 us (1%)
    reduce_scatter x2, waiting for transfers between devices, apply_graph(): lax.psum_scatter(col_totals.reshape(vec_width, -1), 'row', scatter_dimens...  187 us
    reduce_scatter x2, waiting for transfers between devices, apply_graph(): lax.psum_scatter(row_totals.reshape(vec_width, -1), 'col', scatter_dimens...  165 us
    scatter-add x14, other arithmetic, turn(): row_totals.at[:, row_index].add(forward)  158 us
    psum x1, waiting for transfers between devices, per_device(): lax.psum((product(basis, images), product(basis, basis)), ('row', 'col'))  148 us
    scatter-add x14, other arithmetic, turn(): col_totals.at[:, col_index].add(backward)  125 us
    all_gather x2, waiting for transfers between devices, apply_graph(): row_range = lax.all_gather(vectors, 'col', axis=1, tiled=True)  71.4 us
    psum x1, blocking collectives, per_device(): gram_x = lax.psum(product(block_x, block_x), ('row', 'col'))  68.9 us
    psum x1, blocking collectives, per_device(): rayleigh = lax.psum(product(orthonormal, image_x), ('row', 'col'))  65.7 us
  transfers between devices with their start and end apart: 8, of which 8 were waited for; matrix products, arithmetic and copies ran while one was open for 1% of the time, Pallas kernels for 0%

commit v1 on v0

--- a/solution.py
+++ b/solution.py
@@ -3,12 +3,36 @@
 import jax.numpy as jnp
 from jax import lax
 from jax.sharding import PartitionSpec as P
+from jax.lax import axis_index, axis_size, ppermute
+
+
+def write_pipes(my_tile, axis_k):
+    g_now = list(my_tile.shape[1:])
+    g_now[axis_k] *= my_tile.shape[0]
+    oldest = jnp.moveaxis(my_tile, 0, axis_k).reshape(g_now)
+    return oldest
+
+
+def columns_read(message, bus_axis, pos_dim=1):
+    seen = []
+    total_devices = axis_size(bus_axis)
+    for pp in range(total_devices):
+        seen.append((pp, (pp + 1) % total_devices))
+    gallery = [message]
+    while len(gallery) < total_devices:
+        tall = ppermute(gallery[-1], axis_name=bus_axis, perm=seen)
+        gallery.append(tall)
+    p_next = axis_index(bus_axis)
+    mixed_arr = jnp.stack(gallery)
+    gallery = mixed_arr[(p_next - jnp.arange(total_devices)) % total_devices]
+    known = write_pipes(gallery, pos_dim)
+    return known
 
 
 def apply_graph(vectors, tile_rows, tile_cols, live_count, tile_vals):
     vec_width = vectors.shape[0]
     tile_size = tile_vals.shape[-1]
-    row_range = lax.all_gather(vectors, "col", axis=1, tiled=True)
+    row_range = columns_read(vectors, "col")
     col_group = lax.all_gather(vectors, "row", axis=1, tiled=True)
     row_blocks = row_range.reshape(vec_width, -1, tile_size)
     col_blocks = col_group.reshape(vec_width, -1, tile_size)

time: 1310 us -> 1470 us (1.12)
  waiting for transfers between devices: 591 us -> 720 us
  local copies, waits for them, and re-layouts: 118 us -> 147 us
    ppermute x0 -> x30, waiting for transfers between devices: none -> 205 us  [columns_read(): tall = ppermute(gallery[-1], axis_name=bus_axis, perm=seen)]
    all_gather x2 -> x0, waiting for transfers between devices: 71.4 us -> none  [apply_graph(): row_range = lax.all_gather(vectors, 'col', axis=1, tiled=True)]
    all_gather x1, waiting for transfers between devices: 19.8 us -> 0.01 us  [apply_graph(): col_group = lax.all_gather(vectors, 'row', axis=1, tiled=True)]
    unnamed x26 -> x54, local copies, waits for them, and re-layouts: 16.6 us -> 34.5 us
    reduce_scatter x2, waiting for transfers between devices: 187 us -> 202 us  [apply_graph(): lax.psum_scatter(col_totals.reshape(vec_width, -1), 'row', scatter_dimens...]
  transfers between devices with their start and end apart: 8 -> 36, of which waited for: 8 -> 35; matrix products, arithmetic and copies ran while one was open for 1% -> 2% of each run, Pallas kernels for 0% -> 0%
where the time goes in v1:
time: 1470 us; the launch traced here: 1460 us
  waiting for transfers between devices  720 us (49%)
  other arithmetic  313 us (21%)
  blocking collectives  148 us (10%)
  local copies, waits for them, and re-layouts  147 us (10%)
  matrix products  119 us (8%)
  between operations  15.1 us (1%)
    ppermute x30, waiting for transfers between devices, columns_read(): tall = ppermute(gallery[-1], axis_name=bus_axis, perm=seen)  205 us
    reduce_scatter x2, waiting for transfers between devices, apply_graph(): lax.psum_scatter(col_totals.reshape(vec_width, -1), 'row', scatter_dimens...  202 us
    reduce_scatter x2, waiting for transfers between devices, apply_graph(): lax.psum_scatter(row_totals.reshape(vec_width, -1), 'col', scatter_dimens...  165 us
    scatter-add x14, other arithmetic, turn(): row_totals.at[:, row_index].add(forward)  160 us
    psum x1, waiting for transfers between devices, per_device(): lax.psum((product(basis, images), product(basis, basis)), ('row', 'col'))  148 us
    scatter-add x14, other arithmetic, turn(): col_totals.at[:, col_index].add(backward)  126 us
    psum x1, blocking collectives, per_device(): gram_x = lax.psum(product(block_x, block_x), ('row', 'col'))  68.9 us
    psum x1, blocking collectives, per_device(): rayleigh = lax.psum(product(orthonormal, image_x), ('row', 'col'))  65.5 us
  transfers between devices with their start and end apart: 36, of which 35 were waited for; matrix products, arithmetic and copies ran while one was open for 2% of the time, Pallas kernels for 0%

profile of v1, /device:TPU:1, one launch (start us, length us, event | category | flops | bytes accessed | tf_op | source)
XLA Modules:
  0.0 1463.1 jit_solution(14774851907993834700)
XLA Ops:
  8.4 68.9 %psum.28 = f32[64,64]{0,1:T(8,128)S(1)} all-reduce(f32[64,64]{0,1:T(8,128)S(1)} %convolution_multiply_fusion.3), channel_id=1, replica_groups=mesh['row'=8,'col'=16] {'row','col'}, use_global_device_ids=true, to_apply=%region_0.0 | all-reduce | flops 4096 | bytes 32768 | tf_op jit(solution)/shard_map/psum | solution.py:90
  149.5 9.4 collective-permute-done.7
  230.9 291.5 %while.26 = (s32[]{:T(128)}, f32[128,96,128]{2,0,1:T(8,128)}, f32[128,48,128]{2,0,1:T(8,128)S(1)}, s32[]{:T(128)}, s32[576]{0:T(1024)S(1)}, /*index=5*/s32[]{:T(...) while((s32[]{:T(128)}, f32[128,96,128]{2,0,1:T(8,128)}, ...), condition=%wide.region_6.7_spmd.clone, body=%wide.region_3.6_spmd.clone.sunk | while | flops 543165312 | bytes 50343056 | solution.py:65
  241.2 13.6 scatter_fusion
  282.8 13.7 scatter_fusion
  324.4 13.7 scatter_fusion
  366.1 13.7 scatter_fusion
  407.8 13.7 scatter_fusion
  449.4 13.6 scatter_fusion
  491.0 13.6 scatter_fusion
  530.6 115.1 %reduce-scatter.7.cloned.1.call-done = f32[128,768]{1,0:T(8,128)} async-done(((f32[128,6144]{1,0:T(8,128)}), f32[128,768]{1,0:T(8,128)}) %reduce-scatter.7.cloned.1.call-update) | async-done | bytes 393232 | tf_op jit(solution)/shard_map/reduce_scatter | solution.py:69
  645.7 85.5 %reduce-scatter.5.cloned.1.call-done = f32[128,768]{1,0:T(8,128)} async-done(((f32[128,12288]{1,0:T(8,128)}), f32[128,768]{1,0:T(8,128)}) %reduce-scatter.5.cloned.1.call-update) | async-done | bytes 393232 | tf_op jit(solution)/shard_map/reduce_scatter | solution.py:66
  732.7 65.5 %psum.29 = f32[64,64]{0,1:T(8,128)S(1)} all-reduce(f32[64,64]{0,1:T(8,128)S(1)} %convolution_multiply_fusion.2), channel_id=1, replica_groups=mesh['row'=8,'col'=16] {'row','col'}, use_global_device_ids=true, to_apply=%region_9.10 | all-reduce | flops 4096 | bytes 32768 | tf_op jit(solution)/shard_map/psum | solution.py:100
  799.2 14.0 all_gather.7
  928.6 200.9 %while.27 = (s32[]{:T(128)}, f32[64,96,128]{2,0,1:T(8,128)}, f32[64,48,128]{2,0,1:T(8,128)}, s32[]{:T(128)}, s32[576]{0:T(1024)S(1)}, /*index=5*/s32[]{:T(128)},...) while((s32[]{:T(128)}, f32[64,96,128]{2,0,1:T(8,128)}, ...), condition=%wide.region_13.14_spmd.clone, body=%wide.region_10.13_spmd.clone.sunk | while | flops 272632704 | bytes 27274384 | solution.py:65
  934.4 9.1 scatter_fusion.2
  948.0 9.2 scatter_fusion.3
  963.0 9.1 scatter_fusion.2
  976.7 9.2 scatter_fusion.3
  991.7 9.1 scatter_fusion.2
  1005.3 9.2 scatter_fusion.3
  1020.3 9.2 scatter_fusion.2
  1034.1 9.4 scatter_fusion.3
  1049.3 9.3 scatter_fusion.2
  1063.1 9.1 scatter_fusion.3
  1078.0 9.1 scatter_fusion.2
  1091.6 9.1 scatter_fusion.3
  1106.6 9.1 scatter_fusion.2
  1120.2 9.2 scatter_fusion.3
  1136.6 87.0 %reduce-scatter.11.cloned.1.call-done = f32[64,768]{1,0:T(8,128)} async-done(((f32[64,6144]{1,0:T(8,128)}), f32[64,768]{1,0:T(8,128)}) %reduce-scatter.11.cloned.1.call-update) | async-done | bytes 196624 | tf_op jit(solution)/shard_map/reduce_scatter | solution.py:69
  1223.6 79.0 %reduce-scatter.9.cloned.1.call-done = f32[64,768]{1,0:T(8,128)} async-done(((f32[64,12288]{1,0:T(8,128)}), f32[64,768]{1,0:T(8,128)}) %reduce-scatter.9.cloned.1.call-update) | async-done | bytes 196624 | tf_op jit(solution)/shard_map/reduce_scatter | solution.py:66
  1305.0 148.0 %all-reduce.3.cloned.1.call-done = (f32[192,192]{1,0:T(8,128)}, f32[192,192]{1,0:T(8,128)}) async-done(((f32[192,192]{1,0:T(8,128)}, f32[192,192]{1,0:T(8,128)}), (f32[192,192]{1,0:T(8,128)}, f32[192,192]{1,0:T(8,128)})) %all-reduce.3.cloned.1.call-update) | async-done | bytes 294928 | tf_op jit(solution)/shard_map/psum | solution.py:108
  (283 shorter events, 550.6 us)
Async XLA Ops:
  7.2 193.6 %all-gather.2.cloned.1.call-start = ((), (), s32[]{:S(2)}) async-start(), calls=%async_computation.4 | async-start | bytes 1769472 | tf_op jit(solution)/shard_map/all_gather | solution.py:36
  91.5 554.1 %reduce-scatter.7.cloned.1.call-start = ((), (), s32[]{:S(2)}) async-start(), calls=%async_computation.6 | async-start | bytes 3538944 | tf_op jit(solution)/shard_map/reduce_scatter | solution.py:69
  91.6 9.2 collective-permute-start
  100.7 7.8 collective-permute-start.1
  108.6 7.8 collective-permute-start.2
  116.4 7.8 collective-permute-start.3
  124.2 7.8 collective-permute-start.4
  132.1 7.8 collective-permute-start.5
  139.9 8.9 collective-permute-start.6
  148.9 10.1 collective-permute-start.7
  159.0 9.3 collective-permute-start.8
  168.2 8.3 collective-permute-start.9
  176.6 7.8 collective-permute-start.10
  184.4 7.8 collective-permute-start.11
  192.3 7.8 collective-permute-start.12
  200.1 7.8 collective-permute-start.13
  207.9 8.3 collective-permute-start.14
  524.4 206.8 %reduce-scatter.5.cloned.1.call-start = ((), (), s32[]{:S(2)}) async-start(), calls=%async_computation.5 | async-start | bytes 6684672 | tf_op jit(solution)/shard_map/reduce_scatter | solution.py:66
  530.5 693.1 %reduce-scatter.11.cloned.1.call-start = ((), (), s32[]{:S(2)}) async-start(), calls=%async_computation.8 | async-start | bytes 1769472 | tf_op jit(solution)/shard_map/reduce_scatter | solution.py:69
  813.2 7.6 collective-permute-start.15
  820.8 6.8 collective-permute-start.16
  834.4 6.8 collective-permute-start.18
  841.2 6.8 collective-permute-start.19
  854.7 7.1 collective-permute-start.21
  861.8 7.8 collective-permute-start.22
  869.6 6.8 collective-permute-start.23
  890.0 6.8 collective-permute-start.26
  896.8 6.8 collective-permute-start.27
  903.6 6.8 collective-permute-start.28
  910.4 8.0 collective-permute-start.29
  1132.3 170.3 %reduce-scatter.9.cloned.1.call-start = ((), (), s32[]{:S(2)}) async-start(), calls=%async_computation.7 | async-start | bytes 3342336 | tf_op jit(solution)/shard_map/reduce_scatter | solution.py:66
  1134.2 318.8 %all-reduce.3.cloned.1.call-start = ((), (), s32[]{:S(2)}) async-start(), calls=%async_computation.9 | async-start | bytes 786432 | tf_op jit(solution)/shard_map/psum | solution.py:108
  (14 other events, 781.9 us)
Sparse Core Ops, SparseCore 0:
  91.6 21.1 all-gather.1
  524.5 121.1 reduce-scatter.6
  649.1 82.0 reduce-scatter.4
  1132.4 91.1 reduce-scatter.10
  1226.8 75.7 reduce-scatter.8
  1307.8 145.1 all-reduce.2
